TPU v7x, 32 devices: a whole 2x2x4 slice. The times are simulated.
32 devices in a mesh: group: 2 (over y), ctx: 4 (over z), head: 2 (over x), pool: 2 (over core).
Axes of the slice: x: 2, y: 2, z: 4, core: 2. Of those that a mesh axis runs over, the one named last changes fastest.
Arguments:
- queries: bfloat16 [1024, 8192], P(('group', 'ctx'), ('head', 'pool')), parts along dimension 0, may hold values from -100 to 100
- new_kv: bfloat16 [2, 1024, 1024], P(None, ('group', 'ctx'), ('head', 'pool')), parts along dimension 1, may hold values from -5 to 5
- pool: bfloat16 [2, 64, 128, 1024], P(None, ('group', 'ctx'), None, ('head', 'pool')), parts along dimension 1, may hold values from -4.5 to 4.5
- block_table: int32 [64], P('group'), parts along dimension 0, may hold values from 0 to 31, as said below
- span_order: int32 [8], P('group'), parts along dimension 0, may hold values from 0 to 3, each once
Outputs:
- attended: bfloat16 [1024, 8192], P(('group', 'ctx'), ('head', 'pool')), parts along dimension 0
There are 2 independent parts, one for each index of `group`. A program takes and returns all parts, laid end to end along the dimension named above; each array names one. Nothing has to cross between parts.
Inputs may be any that keep to these rules, and one draw needn't show every extreme that they name: `block_table`: all ids differ. Index h of ctx holds pool ids h * 8 to (h + 1) * 8 - 1. In each aligned group of 8 entries (entries k * 8 to (k + 1) * 8 - 1), every index of ctx holds either none or exactly 2 of the ids.
All inputs are finite; a program needn't handle non-finite values.
Results may differ from a plain program's by a relative error of at most 0.0045.
Values may be sent and summed in bfloat16 or wider, within the bound.
A program may use at most 128 MiB of HBM per device.

v0:
```python
import math

import jax
import jax.numpy as jnp
from jax import lax
from jax.sharding import PartitionSpec as P

HD = 128
QH = 64
KVH = 8
CAP = 2


masked_score = -1e30


def lookup(indices, table):
    slots = jnp.arange(table.shape[0], dtype=jnp.int32)
    return jnp.sum(jnp.where(indices[:, None] == slots[None, :], table[None, :], 0), axis=1)


def key_positions(row_count, resident_rows, prefix_rows_dev, span_order, queries_dev, prefix_total):
    global_row = jnp.arange(row_count, dtype=jnp.int32)
    owner_index = global_row // resident_rows
    offset = global_row - owner_index * resident_rows
    span_index = lookup(owner_index, span_order)
    from_new = prefix_total + span_index * queries_dev + offset - prefix_rows_dev
    return jnp.where(offset < prefix_rows_dev, owner_index * prefix_rows_dev + offset, from_new)


def attend(state_now, query_rows, query_pos, kv_piece, key_pos, score_scale):
    acc_out, acc_max, acc_sum = state_now
    kv_heads = query_rows.shape[0]
    head_dim = query_rows.shape[2]
    row_count = kv_piece.shape[1]
    key_block = kv_piece[0].reshape(row_count, kv_heads, head_dim)
    value_block = kv_piece[1].reshape(row_count, kv_heads, head_dim)
    scores = (
        lax.dot_general(
            query_rows, key_block, (((2,), (2,)), ((0,), (1,))), preferred_element_type=jnp.float32
        )
        * score_scale
    )
    allowed = key_pos[None, None, :] <= query_pos[None, :, None]
    scores = jnp.where(allowed, scores, masked_score)
    new_max = jnp.maximum(acc_max, jnp.max(scores, axis=2))
    correct = jnp.exp(acc_max - new_max)
    exp_scores = jnp.where(allowed, jnp.exp(scores - new_max[:, :, None]), 0.0)
    new_sum = acc_sum * correct + jnp.sum(exp_scores, axis=2)
    weights = exp_scores.astype(jnp.bfloat16)
    update = lax.dot_general(
        weights, value_block, (((2,), (0,)), ((0,), (1,))), preferred_element_type=jnp.float32
    )
    return (acc_out * correct[:, :, None] + update, new_max, new_sum)


def attend_piece(state_now, query_rows, query_pos, kv_piece, key_pos, score_scale):
    row_count = kv_piece.shape[1]
    block_rows = row_count
    while block_rows > 2048 and block_rows % 2 == 0:
        block_rows = block_rows // 2
    block_count = row_count // block_rows
    blocks = jnp.moveaxis(kv_piece.reshape(2, block_count, block_rows, kv_piece.shape[2]), 1, 0)
    positions = key_pos.reshape(block_count, block_rows)

    def one_block(state_inner, block_item):
        return (
            attend(state_inner, query_rows, query_pos, block_item[0], block_item[1], score_scale),
            None,
        )

    final_state, unused = lax.scan(one_block, state_now, (blocks, positions))
    return final_state


def local(queries, new_kv, pool, block_table, span_order):
    cycle_size = lax.axis_size("ctx")
    my_index = lax.axis_index("ctx")
    per_group = QH // KVH
    queries_dev = queries.shape[0]
    kv_heads = new_kv.shape[2] // HD
    pool_dev = pool.shape[1]
    block_len = pool.shape[2]
    blocks_dev = block_table.shape[0] // cycle_size
    owner_table = block_table.reshape(cycle_size, blocks_dev)
    holder = owner_table // pool_dev
    local_id = owner_table - holder * pool_dev
    same_holder = holder[:, :, None] == holder[:, None, :]
    earlier = (
        jnp.arange(blocks_dev, dtype=jnp.int32)[:, None]
        < jnp.arange(blocks_dev, dtype=jnp.int32)[None, :]
    )
    rank_in_list = jnp.sum((same_holder & earlier[None, :, :]).astype(jnp.int32), axis=1)
    slot_match = (holder[:, None, :] == my_index) & (
        rank_in_list[:, None, :] == jnp.arange(CAP, dtype=jnp.int32)[None, :, None]
    )
    source = jnp.sum(jnp.where(slot_match, local_id[:, None, :], 0), axis=2)
    filled = jnp.any(slot_match, axis=2)
    picked = jnp.take(pool, source.reshape(-1), axis=1)
    picked = jnp.where(filled.reshape(1, -1, 1, 1), picked, jnp.zeros_like(picked))
    outgoing = picked.reshape(2, cycle_size, CAP, block_len, pool.shape[3])
    incoming = lax.all_to_all(outgoing, "ctx", split_axis=1, concat_axis=1, tiled=True)
    my_holder = lax.dynamic_index_in_dim(holder, my_index, 0, keepdims=False)
    my_rank = lax.dynamic_index_in_dim(rank_in_list, my_index, 0, keepdims=False)
    flat_slot = my_holder * CAP + my_rank
    arrived = incoming.reshape(2, cycle_size * CAP, block_len, pool.shape[3])
    prefix_kv = jnp.take(arrived, flat_slot, axis=1).reshape(
        2, blocks_dev * block_len, pool.shape[3]
    )
    resident = jnp.concatenate([prefix_kv, new_kv], axis=1)
    resident_rows = resident.shape[1]
    prefix_rows_dev = blocks_dev * block_len
    prefix_total = cycle_size * prefix_rows_dev
    score_scale = 1.0 / math.sqrt(HD)
    row_offsets = jnp.arange(queries_dev, dtype=jnp.int32)
    own_span = lookup(my_index[None], span_order)[0]
    own_pos = jnp.repeat(prefix_total + own_span * queries_dev + row_offsets, per_group)
    query_rows = (
        queries.reshape(queries_dev, kv_heads, per_group, HD)
        .transpose(1, 0, 2, 3)
        .reshape(kv_heads, queries_dev * per_group, HD)
    )
    grouped_rows = queries_dev * per_group
    start_state = (
        jnp.zeros((kv_heads, grouped_rows, HD), jnp.float32),
        jnp.full((kv_heads, grouped_rows), masked_score, jnp.float32),
        jnp.zeros((kv_heads, grouped_rows), jnp.float32),
    )
    kv_piece = lax.all_gather(resident, "ctx", axis=1, tiled=True)
    positions = key_positions(
        kv_piece.shape[1], resident_rows, prefix_rows_dev, span_order, queries_dev, prefix_total
    )
    final_state = attend_piece(start_state, query_rows, own_pos, kv_piece, positions, score_scale)
    out_sum, out_max, out_total = final_state
    result = out_sum / out_total[:, :, None]
    result = (
        result.reshape(kv_heads, queries_dev, per_group, HD)
        .transpose(1, 0, 2, 3)
        .reshape(queries_dev, kv_heads * per_group * HD)
    )
    return result.astype(jnp.bfloat16)


def solution(mesh):
    return jax.shard_map(
        local,
        mesh=mesh,
        in_specs=(
            P(("group", "ctx"), ("head", "pool")),
            P(None, ("group", "ctx"), ("head", "pool")),
            P(None, ("group", "ctx"), None, ("head", "pool")),
            P("group"),
            P("group"),
        ),
        out_specs=P(("group", "ctx"), ("head", "pool")),
        check_vma=False,
    )
```

profile of v0, /device:TPU:0, one launch (start us, length us, event | category | flops | bytes accessed | tf_op | source)
XLA Modules:
  0.0 203.0 jit_solution(7533844916817455313)
XLA Ops:
  9.0 1.1 copy.56
  10.1 6.3 %all-to-all-start = ((bf16[2,4,2,128,256]{4,3,2,0,1:T(8,128)(2,1)}), bf16[2,4,2,128,256]{4,3,2,0,1:T(8,128)(2,1)S(1)}, u32[]{:S(2)}, u32[]{:S(2)}) async-start(bf16[2,4,2,128,256]{4,3,2,0,1:T(8,128)(2,1)} %copy.56), calls=%async_computation | async-start | bytes 2097152 | tf_op jit(solution)/shard_map/all_to_all | solution.py:102
  16.5 25.7 %all-to-all-done = bf16[2,4,2,128,256]{4,3,2,0,1:T(8,128)(2,1)S(1)} async-done(((bf16[2,4,2,128,256]{4,3,2,0,1:T(8,128)(2,1)}), bf16[2,4,2,128,256]{4,3,2,0,1:T(8,128)(2,1)S(1)}, u32[]{:S(2)}, u32[]{:S(2)}) %all-to-all-start) | async-done | bytes 1048608 | tf_op jit(solution)/shard_map/all_to_all | solution.py:102
  43.2 1.1 pad_maximum_fusion
  44.5 1.1 copy.70
  47.8 85.1 %all-gather.2.cloned.1.call-done = bf16[2,4608,256]{2,1,0:T(8,128)(2,1)} async-done(((bf16[2,1152,256]{2,1,0:T(8,128)(2,1)}), bf16[2,4608,256]{2,1,0:T(8,128)(2,1)}) %all-gather.2.cloned.1.call-update) | async-done | bytes 4718608 | tf_op jit(solution)/shard_map/all_gather | solution.py:129
  133.0 60.5 %while.15 = (s32[]{:T(128)}, f32[2,1024,128]{2,1,0:T(8,128)}, f32[2,1024]{1,0:T(2,128)S(1)}, f32[2,1024]{1,0:T(2,128)S(1)}, s32[4,1152]{1,0:T(4,128)S(1)}, /*ind...) while((s32[]{:T(128)}, f32[2,1024,128]{2,1,0:T(8,128)}, ...), condition=%wide.region_8.10_spmd.clone, body=%wide.region_5.9_spmd.clone.sunk | while | flops 1240606720 | bytes 52459752 | solution.py:72
  133.9 1.3 constant_dynamic-slice_fusion.3
  135.3 1.1 copy.78
  136.7 3.4 %fusion.43 = (f32[2,1024]{1,0:T(2,128)S(1)}, f32[2,1152,1024]{2,1,0:T(8,128)S(1)}) fusion(pred[1024,1152]{0,1:T(8,128)(4,1)S(1)} %broadcast_compare_fusion.3, bf16[1152,2,128]{0,2,1:T(8,128)(2,1)S(1)} %bitcast.64, bf16[2,1024,128]{2,1,0:T(8,128)(2,1)} %get-tuple-element.244), kind=kOutput, calls=%fused_computation.5.clone.1 | convolution fusion | flops 611055616 | bytes 11739136 | tf_op jit(solution)/shard_map/while/body/eval_jaxpr/dot_general | solution.py:39
  140.0 2.5 %fusion.45 = f32[2,1024]{1,0:T(2,128)S(1)} fusion(f32[2,1152,1024]{2,1,0:T(8,128)S(1)} %get-tuple-element.212, f32[2,1024]{1,0:T(2,128)S(1)} %fusion.44, pred[1024,1152]{0,1:T(8,128)(4,1)S(1)} %broadcast_compare_fusion.3), kind=kLoop, calls=%fused_computation.6.clone.1 | loop fusion | flops 11794432 | bytes 10633216 | tf_op jit(solution)/shard_map/while/body/eval_jaxpr/reduce_sum | solution.py:49
  142.6 4.5 %fusion.47 = f32[2,1024,128]{2,1,0:T(8,128)S(1)} fusion(bf16[1152,2,128]{0,2,1:T(8,128)(2,1)S(1)} %bitcast.63, f32[2,1152,1024]{2,1,0:T(8,128)S(1)} %get-tuple-element.212, f32[2,1024]{1,0:T(2,128)S(1)} %fusion.44, pred[1024,1152]{0,1:T(8,128)(4,1)S(1)} %broadcast_compare_fusion.3, f32[2,1024,128]{2,1,0:T(8,128)S(1)} %copy-done.2, ...), kind=kOutput, calls=%fused_computation.11.clone.1 | convolution fusion | flops 616562688 | bytes 13320193 | tf_op jit(solution)/shard_map/while/body/eval_jaxpr/dot_general | solution.py:51
  147.1 1.0 copy-done.3
  149.1 1.3 constant_dynamic-slice_fusion.3
  150.4 1.1 copy.78
  151.8 3.4 %fusion.43 = (f32[2,1024]{1,0:T(2,128)S(1)}, f32[2,1152,1024]{2,1,0:T(8,128)S(1)}) fusion(pred[1024,1152]{0,1:T(8,128)(4,1)S(1)} %broadcast_compare_fusion.3, bf16[1152,2,128]{0,2,1:T(8,128)(2,1)S(1)} %bitcast.64, bf16[2,1024,128]{2,1,0:T(8,128)(2,1)} %get-tuple-element.244), kind=kOutput, calls=%fused_computation.5.clone.1 | convolution fusion | flops 611055616 | bytes 11739136 | tf_op jit(solution)/shard_map/while/body/eval_jaxpr/dot_general | solution.py:39
  155.2 2.5 %fusion.45 = f32[2,1024]{1,0:T(2,128)S(1)} fusion(f32[2,1152,1024]{2,1,0:T(8,128)S(1)} %get-tuple-element.212, f32[2,1024]{1,0:T(2,128)S(1)} %fusion.44, pred[1024,1152]{0,1:T(8,128)(4,1)S(1)} %broadcast_compare_fusion.3), kind=kLoop, calls=%fused_computation.6.clone.1 | loop fusion | flops 11794432 | bytes 10633216 | tf_op jit(solution)/shard_map/while/body/eval_jaxpr/reduce_sum | solution.py:49
  157.7 4.5 %fusion.47 = f32[2,1024,128]{2,1,0:T(8,128)S(1)} fusion(bf16[1152,2,128]{0,2,1:T(8,128)(2,1)S(1)} %bitcast.63, f32[2,1152,1024]{2,1,0:T(8,128)S(1)} %get-tuple-element.212, f32[2,1024]{1,0:T(2,128)S(1)} %fusion.44, pred[1024,1152]{0,1:T(8,128)(4,1)S(1)} %broadcast_compare_fusion.3, f32[2,1024,128]{2,1,0:T(8,128)S(1)} %copy-done.2, ...), kind=kOutput, calls=%fused_computation.11.clone.1 | convolution fusion | flops 616562688 | bytes 13320193 | tf_op jit(solution)/shard_map/while/body/eval_jaxpr/dot_general | solution.py:51
  162.3 1.0 copy-done.3
  164.2 1.3 constant_dynamic-slice_fusion.3
  165.5 1.1 copy.78
  166.9 3.4 %fusion.43 = (f32[2,1024]{1,0:T(2,128)S(1)}, f32[2,1152,1024]{2,1,0:T(8,128)S(1)}) fusion(pred[1024,1152]{0,1:T(8,128)(4,1)S(1)} %broadcast_compare_fusion.3, bf16[1152,2,128]{0,2,1:T(8,128)(2,1)S(1)} %bitcast.64, bf16[2,1024,128]{2,1,0:T(8,128)(2,1)} %get-tuple-element.244), kind=kOutput, calls=%fused_computation.5.clone.1 | convolution fusion | flops 611055616 | bytes 11739136 | tf_op jit(solution)/shard_map/while/body/eval_jaxpr/dot_general | solution.py:39
  170.3 2.5 %fusion.45 = f32[2,1024]{1,0:T(2,128)S(1)} fusion(f32[2,1152,1024]{2,1,0:T(8,128)S(1)} %get-tuple-element.212, f32[2,1024]{1,0:T(2,128)S(1)} %fusion.44, pred[1024,1152]{0,1:T(8,128)(4,1)S(1)} %broadcast_compare_fusion.3), kind=kLoop, calls=%fused_computation.6.clone.1 | loop fusion | flops 11794432 | bytes 10633216 | tf_op jit(solution)/shard_map/while/body/eval_jaxpr/reduce_sum | solution.py:49
  172.9 4.5 %fusion.47 = f32[2,1024,128]{2,1,0:T(8,128)S(1)} fusion(bf16[1152,2,128]{0,2,1:T(8,128)(2,1)S(1)} %bitcast.63, f32[2,1152,1024]{2,1,0:T(8,128)S(1)} %get-tuple-element.212, f32[2,1024]{1,0:T(2,128)S(1)} %fusion.44, pred[1024,1152]{0,1:T(8,128)(4,1)S(1)} %broadcast_compare_fusion.3, f32[2,1024,128]{2,1,0:T(8,128)S(1)} %copy-done.2, ...), kind=kOutput, calls=%fused_computation.11.clone.1 | convolution fusion | flops 616562688 | bytes 13320193 | tf_op jit(solution)/shard_map/while/body/eval_jaxpr/dot_general | solution.py:51
  177.4 1.0 copy-done.3
  179.3 1.3 constant_dynamic-slice_fusion.3
  180.6 1.1 copy.78
  182.0 3.4 %fusion.43 = (f32[2,1024]{1,0:T(2,128)S(1)}, f32[2,1152,1024]{2,1,0:T(8,128)S(1)}) fusion(pred[1024,1152]{0,1:T(8,128)(4,1)S(1)} %broadcast_compare_fusion.3, bf16[1152,2,128]{0,2,1:T(8,128)(2,1)S(1)} %bitcast.64, bf16[2,1024,128]{2,1,0:T(8,128)(2,1)} %get-tuple-element.244), kind=kOutput, calls=%fused_computation.5.clone.1 | convolution fusion | flops 611055616 | bytes 11739136 | tf_op jit(solution)/shard_map/while/body/eval_jaxpr/dot_general | solution.py:39
  185.4 2.5 %fusion.45 = f32[2,1024]{1,0:T(2,128)S(1)} fusion(f32[2,1152,1024]{2,1,0:T(8,128)S(1)} %get-tuple-element.212, f32[2,1024]{1,0:T(2,128)S(1)} %fusion.44, pred[1024,1152]{0,1:T(8,128)(4,1)S(1)} %broadcast_compare_fusion.3), kind=kLoop, calls=%fused_computation.6.clone.1 | loop fusion | flops 11794432 | bytes 10633216 | tf_op jit(solution)/shard_map/while/body/eval_jaxpr/reduce_sum | solution.py:49
  188.0 4.5 %fusion.47 = f32[2,1024,128]{2,1,0:T(8,128)S(1)} fusion(bf16[1152,2,128]{0,2,1:T(8,128)(2,1)S(1)} %bitcast.63, f32[2,1152,1024]{2,1,0:T(8,128)S(1)} %get-tuple-element.212, f32[2,1024]{1,0:T(2,128)S(1)} %fusion.44, pred[1024,1152]{0,1:T(8,128)(4,1)S(1)} %broadcast_compare_fusion.3, f32[2,1024,128]{2,1,0:T(8,128)S(1)} %copy-done.2, ...), kind=kOutput, calls=%fused_computation.11.clone.1 | convolution fusion | flops 616562688 | bytes 13320193 | tf_op jit(solution)/shard_map/while/body/eval_jaxpr/dot_general | solution.py:51
  192.5 1.0 copy-done.3
  193.5 1.6 fusion.16
  (95 shorter events, 11.2 us)
Async XLA Ops:
  6.5 1.7 copy-start
  6.5 36.6 %copy-start.4 = (bf16[2,128,256]{2,1,0:T(8,128)(2,1)S(1)}, bf16[2,128,256]{2,1,0:T(8,128)(2,1)}, u32[]{:S(2)}) copy-start(bf16[2,128,256]{2,1,0:T(8,128)(2,1)} %param.10) | copy-start | bytes 393220
  8.8 35.5 %copy-start.5 = (s32[4]{0:T(128)S(1)}, s32[4]{0:T(128)}, u32[]{:S(2)}) copy-start(s32[4]{0:T(128)} %param.13) | copy-start | bytes 52
  10.1 32.0 %all-to-all-start = ((bf16[2,4,2,128,256]{4,3,2,0,1:T(8,128)(2,1)}), bf16[2,4,2,128,256]{4,3,2,0,1:T(8,128)(2,1)S(1)}, u32[]{:S(2)}, u32[]{:S(2)}) async-start(bf16[2,4,2,128,256]{4,3,2,0,1:T(8,128)(2,1)} %copy.56), calls=%async_computation | async-start | bytes 2097152 | tf_op jit(solution)/shard_map/all_to_all | solution.py:102
  16.4 116.5 %all-gather.2.cloned.1.call-start = ((), (), s32[]{:S(2)}) async-start(), calls=%async_computation.1 | async-start | bytes 5898240 | tf_op jit(solution)/shard_map/all_gather | solution.py:129
  136.6 6.0 %copy-start.1 = (bf16[1,1,1152,256]{2,3,1,0:T(8,128)(2,1)S(1)}, bf16[1,1,1152,256]{2,3,1,0:T(8,128)(2,1)}, u32[]{:S(2)}) copy-start(bf16[1,1,1152,256]{2,3,1,0:T(8,128)(2,1)} %copy.78) | copy-start | bytes 1769476 | tf_op jit(solution)/shard_map/while
  136.6 6.0 %copy-start.2 = (f32[2,1024,128]{2,1,0:T(8,128)S(1)}, f32[2,1024,128]{2,1,0:T(8,128)}, u32[]{:S(2)}) copy-start(f32[2,1024,128]{2,1,0:T(8,128)} %get-tuple-element.228) | copy-start | bytes 3145732 | tf_op jit(solution)/shard_map/while
  147.1 1.0 copy-start.3
  151.8 6.0 %copy-start.1 = (bf16[1,1,1152,256]{2,3,1,0:T(8,128)(2,1)S(1)}, bf16[1,1,1152,256]{2,3,1,0:T(8,128)(2,1)}, u32[]{:S(2)}) copy-start(bf16[1,1,1152,256]{2,3,1,0:T(8,128)(2,1)} %copy.78) | copy-start | bytes 1769476 | tf_op jit(solution)/shard_map/while
  151.8 6.0 %copy-start.2 = (f32[2,1024,128]{2,1,0:T(8,128)S(1)}, f32[2,1024,128]{2,1,0:T(8,128)}, u32[]{:S(2)}) copy-start(f32[2,1024,128]{2,1,0:T(8,128)} %get-tuple-element.228) | copy-start | bytes 3145732 | tf_op jit(solution)/shard_map/while
  162.2 1.0 copy-start.3
  166.9 6.0 %copy-start.1 = (bf16[1,1,1152,256]{2,3,1,0:T(8,128)(2,1)S(1)}, bf16[1,1,1152,256]{2,3,1,0:T(8,128)(2,1)}, u32[]{:S(2)}) copy-start(bf16[1,1,1152,256]{2,3,1,0:T(8,128)(2,1)} %copy.78) | copy-start | bytes 1769476 | tf_op jit(solution)/shard_map/while
  166.9 6.0 %copy-start.2 = (f32[2,1024,128]{2,1,0:T(8,128)S(1)}, f32[2,1024,128]{2,1,0:T(8,128)}, u32[]{:S(2)}) copy-start(f32[2,1024,128]{2,1,0:T(8,128)} %get-tuple-element.228) | copy-start | bytes 3145732 | tf_op jit(solution)/shard_map/while
  177.4 1.0 copy-start.3
  182.0 6.0 %copy-start.1 = (bf16[1,1,1152,256]{2,3,1,0:T(8,128)(2,1)S(1)}, bf16[1,1,1152,256]{2,3,1,0:T(8,128)(2,1)}, u32[]{:S(2)}) copy-start(bf16[1,1,1152,256]{2,3,1,0:T(8,128)(2,1)} %copy.78) | copy-start | bytes 1769476 | tf_op jit(solution)/shard_map/while
  182.0 6.0 %copy-start.2 = (f32[2,1024,128]{2,1,0:T(8,128)S(1)}, f32[2,1024,128]{2,1,0:T(8,128)}, u32[]{:S(2)}) copy-start(f32[2,1024,128]{2,1,0:T(8,128)} %get-tuple-element.228) | copy-start | bytes 3145732 | tf_op jit(solution)/shard_map/while
  192.5 1.0 copy-start.3
Sparse Core Ops, SparseCore 0:
  44.4 88.5 all-gather.1
where the time goes:
time: 203 us
  waiting for transfers between devices  111 us (55%)
  matrix products  31.4 us (15%)
  local copies, waits for them, and re-layouts  22.3 us (11%)
  other arithmetic  17.5 us (9%)
  between operations  14.2 us (7%)
  starting transfers between devices  6.32 us (3%)
    all_gather x1, waiting for transfers between devices, local(): kv_piece = lax.all_gather(resident, 'ctx', axis=1, tiled=True)  85.1 us
    all_to_all x1, waiting for transfers between devices, local(): lax.all_to_all(outgoing, 'ctx', split_axis=1, concat_axis=1, tiled=True)  25.7 us
    dot_general x4, matrix products, attend(): lax.dot_general(weights, value_block, (((2,), (0,)), ((0,), (1,))), prefe...  18 us
    dot_general x4, matrix products, attend(): lax.dot_general(query_rows, key_block, (((2,), (2,)), ((0,), (1,))), pref...  13.5 us
    reduce_sum x4, other arithmetic, attend(): new_sum = acc_sum * correct + jnp.sum(exp_scores, axis=2)  10.1 us
    while x36, local copies, waits for them, and re-layouts  9.48 us
    all_to_all x1, starting transfers between devices, local(): lax.all_to_all(outgoing, 'ctx', split_axis=1, concat_axis=1, tiled=True)  6.32 us
    slice x4, local copies, waits for them, and re-layouts, attend(): key_block = kv_piece[0].reshape(row_count, kv_heads, head_dim)  5.31 us
  transfers between devices with their start and end apart: 2, of which 2 were waited for; matrix products, arithmetic and copies ran while one was open for 1% of the time, Pallas kernels for 0%

commit v1 on v0

--- a/solution.py
+++ b/solution.py
@@ -1,8 +1,11 @@
+import functools
 import math
 
 import jax
 import jax.numpy as jnp
 from jax import lax
+from jax.experimental import pallas as pl
+from jax.experimental.pallas import tpu as pltpu
 from jax.sharding import PartitionSpec as P
 
 HD = 128
@@ -73,7 +76,7 @@
     return final_state
 
 
-def local(queries, new_kv, pool, block_table, span_order):
+def routed(queries, new_kv, pool, block_table, span_order):
     cycle_size = lax.axis_size("ctx")
     my_index = lax.axis_index("ctx")
     per_group = QH // KVH
@@ -141,6 +144,359 @@
     return result.astype(jnp.bfloat16)
 
 
+def context_kernel(
+    n, kv_heads, per_group, splits, offload,
+    span_ref, queries_ref, new_ref, pool_ref, out_ref,
+    kv, qs, acc, row_max, part_out, part_stat, got_out, got_stat,
+    load_sem, query_sem, send_sem, recv_sem, edge_send, edge_recv,
+):
+    me = lax.axis_index("ctx")
+    pool_dev, block_len = pool_ref.shape[1], pool_ref.shape[2]
+    pieces, group_blocks = kv.shape[1], kv.shape[3]
+    keys = group_blocks * block_len
+    rows = queries_ref.shape[0]
+    tile_heads = 2 if per_group % 2 == 0 else 1
+    tile_rows = tile_heads * rows
+    tiles = per_group // tile_heads
+    unit = math.log2(math.e) / math.sqrt(HD)
+
+    at_edge = (me == 0) | (me == n - 1)
+
+    loads = [[] for _ in range(pieces)]
+    count = 0
+    for piece in range(pieces):
+        kv_head, split = divmod(piece, splits)
+        columns = pl.ds(kv_head * HD, HD)
+        first = split * group_blocks
+        pool_blocks = min(group_blocks, pool_dev - first)
+        for t in range(2):
+            if pool_blocks > 0:
+                loads[piece].append(
+                    pltpu.make_async_copy(
+                        pool_ref.at[t, pl.ds(first, pool_blocks), :, columns],
+                        kv.at[me, piece, t, pl.ds(0, pool_blocks)],
+                        load_sem.at[count],
+                    )
+                )
+                count += 1
+            if pool_blocks < group_blocks:
+                loads[piece].append(
+                    pltpu.make_async_copy(
+                        new_ref.at[t, :, columns],
+                        kv.at[me, piece, t, group_blocks - 1],
+                        load_sem.at[count],
+                    )
+                )
+                count += 1
+    for piece in range(pieces):
+        for load in loads[piece]:
+            load.start()
+    query_loads = []
+    for head in range(kv_heads * per_group):
+        query_loads.append(
+            pltpu.make_async_copy(
+                queries_ref.at[:, pl.ds(head * HD, HD)],
+                qs.at[head // per_group, head % per_group],
+                query_sem.at[head],
+            )
+        )
+        query_loads[-1].start()
+
+    barrier = pltpu.get_barrier_semaphore()
+
+    @pl.when(me > 0)
+    def _():
+        pl.semaphore_signal(
+            barrier, inc=1, device_id={"ctx": me - 1}, device_id_type=pl.DeviceIdType.MESH
+        )
+
+    @pl.when(me < n - 1)
+    def _():
+        pl.semaphore_signal(
+            barrier, inc=1, device_id={"ctx": me + 1}, device_id_type=pl.DeviceIdType.MESH
+        )
+
+    @pl.when(at_edge)
+    def _():
+        pl.semaphore_wait(barrier, 1)
+
+    @pl.when(jnp.logical_not(at_edge))
+    def _():
+        pl.semaphore_wait(barrier, 2)
+
+    def piece_copy(source, piece, side):
+        return pltpu.make_async_remote_copy(
+            src_ref=kv.at[source, piece],
+            dst_ref=kv.at[source, piece],
+            send_sem=send_sem.at[side, source, piece],
+            recv_sem=recv_sem.at[source, piece],
+            device_id={"ctx": me + 2 * side - 1},
+            device_id_type=pl.DeviceIdType.MESH,
+        )
+
+    def edge_copy(index, source, target, device):
+        return pltpu.make_async_remote_copy(
+            src_ref=source,
+            dst_ref=target,
+            send_sem=edge_send.at[index],
+            recv_sem=edge_recv.at[index],
+            device_id={"ctx": device},
+            device_id_type=pl.DeviceIdType.MESH,
+        )
+
+    by_edge = (me == 1) | (me == n - 2)
+    inner = jnp.where(me == 0, 1, n - 2)
+    outer = jnp.where(me == 1, 0, n - 1)
+
+    for piece in range(pieces):
+        for load in loads[piece]:
+            load.wait()
+
+        @pl.when(me > 0)
+        def _():
+            piece_copy(me, piece, 0).start()
+
+        @pl.when(me < n - 1)
+        def _():
+            piece_copy(me, piece, 1).start()
+
+        if offload and piece == splits - 1:
+            for head in range(per_group):
+                query_loads[head].wait()
+
+            @pl.when(at_edge)
+            def _():
+                edge_copy(0, qs.at[0], qs.at[kv_heads], inner).start()
+
+    for head in range(per_group if offload else 0, kv_heads * per_group):
+        query_loads[head].wait()
+
+    acc[...] = jnp.zeros(acc.shape, jnp.float32)
+    row_max[...] = jnp.full(row_max.shape, masked_score, jnp.float32)
+
+    query_row = lax.broadcasted_iota(jnp.int32, (tile_heads, rows, block_len), 1).reshape(
+        tile_rows, block_len
+    )
+    key_column = lax.broadcasted_iota(jnp.int32, (tile_rows, block_len), 1)
+    offset = key_column - query_row
+
+    def attend_tiles(group, source, piece, asker):
+        key_rows = kv[source, piece, 0].reshape(keys, HD)
+        value_rows = kv[source, piece, 1].reshape(keys, HD)
+        value_ones = jnp.concatenate([value_rows, jnp.ones_like(value_rows)], axis=1)
+        has_new = lax.rem(piece, splits) == splits - 1
+        limit = (span_ref[asker] - span_ref[source]) * rows
+        limit = jnp.where(has_new, limit, rows + block_len)
+        allowed = offset <= limit
+        for tile in range(tiles):
+            heads = pl.ds(tile * tile_heads, tile_heads)
+            query_tile = qs[group, heads].reshape(tile_rows, HD)
+            scores = lax.dot_general(
+                query_tile, key_rows, (((1,), (1,)), ((), ())), preferred_element_type=jnp.float32
+            )
+            last = jnp.where(allowed, scores[:, keys - block_len :], masked_score)
+            scores = jnp.concatenate([scores[:, : keys - block_len], last], axis=1)
+            span = pl.ds(tile * tile_rows, tile_rows)
+            old_max = row_max[group, span]
+            new_max = jnp.maximum(old_max, jnp.max(scores, axis=1, keepdims=True))
+            row_max[group, span] = new_max
+            correct = jnp.exp2((old_max - new_max) * unit)
+            wide = jnp.concatenate([new_max] * group_blocks, axis=1)
+            weights = jnp.exp2((scores - wide) * unit).astype(jnp.bfloat16)
+            update = jnp.dot(weights, value_ones, preferred_element_type=jnp.float32)
+            acc[group, span] = (
+                acc[group, span] * jnp.concatenate([correct, correct], axis=1) + update
+            )
+
+    def own_piece(piece, carry):
+        attend_tiles(piece // splits, me, piece, me)
+        return carry
+
+    lax.fori_loop(0, pieces, own_piece, 0)
+
+    if offload:
+
+        @pl.when(by_edge)
+        def _():
+            edge_copy(0, qs.at[0], qs.at[kv_heads], outer).wait_recv()
+
+    diagonal = lax.broadcasted_iota(jnp.int32, (rows, HD), 0) == lax.broadcasted_iota(
+        jnp.int32, (rows, HD), 1
+    )
+
+    def return_part():
+        for head in range(per_group):
+            span = pl.ds(head * rows, rows)
+            total = acc[kv_heads, span, HD:]
+            part_out[head] = (acc[kv_heads, span, :HD] / total).astype(jnp.bfloat16)
+            peak = row_max[kv_heads, span]
+            part_stat[0, pl.ds(head, 1)] = jnp.sum(
+                jnp.where(diagonal, peak, 0.0), axis=0, keepdims=True
+            )
+            part_stat[1, pl.ds(head, 1)] = jnp.sum(
+                jnp.where(diagonal, total, 0.0), axis=0, keepdims=True
+            )
+        edge_copy(1, part_out, got_out, outer).start()
+        edge_copy(2, part_stat, got_stat, outer).start()
+
+    def arrival(step, carry):
+        distance = 1 + step // (2 * pieces)
+        piece = (step % (2 * pieces)) // 2
+        side = step % 2
+        source = me + (1 - 2 * side) * distance
+        onward = me + 2 * side - 1
+        valid = (source >= 0) & (source < n)
+        has_next = (onward >= 0) & (onward < n)
+        if offload:
+            head_off = piece < splits
+            valid = valid & jnp.logical_not(at_edge & head_off & (distance >= 2))
+            handed = has_next & head_off & ((onward == 0) | (onward == n - 1))
+        else:
+            handed = False
+
+        @pl.when(valid)
+        def _():
+            copy = piece_copy(source, piece, side)
+            copy.wait_recv()
+
+            @pl.when(has_next & jnp.logical_not(handed))
+            def _():
+                copy.start()
+
+            if offload:
+
+                @pl.when(handed)
+                def _():
+                    attend_tiles(kv_heads, source, piece, onward)
+
+                    @pl.when((distance == n - 2) & (piece == splits - 1))
+                    def _():
+                        return_part()
+
+            attend_tiles(piece // splits, source, piece, me)
+
+        return carry
+
+    lax.fori_loop(0, 2 * pieces * (n - 1), arrival, 0)
+
+    def settle(group, head):
+        columns = pl.ds((group * per_group + head) * HD, HD)
+        span = pl.ds(head * rows, rows)
+        out_ref[:, columns] = (acc[group, span, :HD] / acc[group, span, HD:]).astype(out_ref.dtype)
+
+    def settle_with_part(head):
+        span = pl.ds(head * rows, rows)
+        their_max = jnp.broadcast_to(got_stat[0, pl.ds(head, 1)], (HD, rows)).T
+        their_total = jnp.broadcast_to(got_stat[1, pl.ds(head, 1)], (HD, rows)).T
+        my_max = row_max[0, span]
+        top = jnp.maximum(my_max, their_max)
+        mine = jnp.exp2((my_max - top) * unit)
+        theirs = jnp.exp2((their_max - top) * unit) * their_total
+        total = acc[0, span, HD:] * mine + theirs
+        summed = acc[0, span, :HD] * mine + got_out[head].astype(jnp.float32) * theirs
+        out_ref[:, pl.ds(head * HD, HD)] = (summed / total).astype(out_ref.dtype)
+
+    for group in range(1 if offload else 0, kv_heads):
+        for head in range(per_group):
+            settle(group, head)
+    if offload:
+
+        @pl.when(at_edge)
+        def _():
+            edge_copy(1, part_out, got_out, inner).wait_recv()
+            edge_copy(2, part_stat, got_stat, inner).wait_recv()
+            for head in range(per_group):
+                settle_with_part(head)
+
+        @pl.when(jnp.logical_not(at_edge))
+        def _():
+            for head in range(per_group):
+                settle(0, head)
+
+    def sent(step, carry):
+        distance = step // (2 * pieces)
+        piece = (step % (2 * pieces)) // 2
+        side = step % 2
+        source = me + (1 - 2 * side) * distance
+        onward = me + 2 * side - 1
+        went = (source >= 0) & (source < n) & (onward >= 0) & (onward < n)
+        if offload:
+            went = went & jnp.logical_not(
+                (distance >= 1) & (piece < splits) & ((onward == 0) | (onward == n - 1))
+            )
+
+        @pl.when(went)
+        def _():
+            piece_copy(source, piece, side).wait_send()
+
+        return carry
+
+    lax.fori_loop(0, 2 * pieces * n, sent, 0)
+    if offload:
+
+        @pl.when(at_edge)
+        def _():
+            edge_copy(0, qs.at[0], qs.at[kv_heads], inner).wait_send()
+
+        @pl.when(by_edge)
+        def _():
+            edge_copy(1, part_out, got_out, outer).wait_send()
+            edge_copy(2, part_stat, got_stat, outer).wait_send()
+
+
+def local(queries, new_kv, pool, block_table, span_order):
+    n = lax.axis_size("ctx")
+    pool_dev, block_len = pool.shape[1], pool.shape[2]
+    rows = queries.shape[0]
+    kv_heads = new_kv.shape[2] // HD
+    per_group = QH // KVH
+    whole_pool = block_table.shape[0] == n * pool_dev
+    if not whole_pool or n < 2 or rows != block_len or rows != HD:
+        return routed(queries, new_kv, pool, block_table, span_order)
+    blocks = pool_dev + 1
+    splits = 3 if blocks % 3 == 0 and blocks > 3 else 1
+    pieces = kv_heads * splits
+    group_blocks = blocks // splits
+    offload = n >= 4 and kv_heads >= 2
+    groups = kv_heads + 1 if offload else kv_heads
+    group_rows = per_group * rows
+    work = queries.shape[1] * rows * block_len * blocks * n
+    return pl.pallas_call(
+        functools.partial(context_kernel, n, kv_heads, per_group, splits, offload),
+        out_shape=jax.ShapeDtypeStruct(queries.shape, jnp.bfloat16),
+        in_specs=[
+            pl.BlockSpec(memory_space=pltpu.SMEM),
+            pl.BlockSpec(memory_space=pl.ANY),
+            pl.BlockSpec(memory_space=pl.ANY),
+            pl.BlockSpec(memory_space=pl.ANY),
+        ],
+        out_specs=pl.BlockSpec(memory_space=pltpu.VMEM),
+        scratch_shapes=[
+            pltpu.VMEM((n, pieces, 2, group_blocks, block_len, HD), jnp.bfloat16),
+            pltpu.VMEM((groups, per_group, rows, HD), jnp.bfloat16),
+            pltpu.VMEM((groups, group_rows, 2 * HD), jnp.float32),
+            pltpu.VMEM((groups, group_rows, HD), jnp.float32),
+            pltpu.VMEM((per_group, rows, HD), jnp.bfloat16),
+            pltpu.VMEM((2, per_group, HD), jnp.float32),
+            pltpu.VMEM((per_group, rows, HD), jnp.bfloat16),
+            pltpu.VMEM((2, per_group, HD), jnp.float32),
+            pltpu.SemaphoreType.DMA((4 * pieces,)),
+            pltpu.SemaphoreType.DMA((kv_heads * per_group,)),
+            pltpu.SemaphoreType.DMA((2, n, pieces)),
+            pltpu.SemaphoreType.DMA((n, pieces)),
+            pltpu.SemaphoreType.DMA((3,)),
+            pltpu.SemaphoreType.DMA((3,)),
+        ],
+        compiler_params=pltpu.CompilerParams(
+            collective_id=0, has_side_effects=True, vmem_limit_bytes=40 * 1024 * 1024
+        ),
+        cost_estimate=pl.CostEstimate(
+            flops=4 * work, bytes_accessed=4 * queries.size, transcendentals=work // HD
+        ),
+        name="context_attention",
+    )(span_order, queries, new_kv, pool)
+
+
 def solution(mesh):
     return jax.shard_map(
         local,

time: 203 us -> 74.6 us (0.37)
  waiting for transfers between devices: 111 us -> 0 us
  Pallas kernels: 0 us -> 69.7 us
  matrix products: 31.4 us -> 0 us
  local copies, waits for them, and re-layouts: 22.3 us -> 4.62 us
  other arithmetic: 17.5 us -> 0 us
  between operations: 14.2 us -> 0.01 us
  starting transfers between devices: 6.32 us -> 0 us
    all_gather x1 -> x0, waiting for transfers between devices: 85.1 us -> none  [local(): kv_piece = lax.all_gather(resident, 'ctx', axis=1, tiled=True)]
    pallas_call x0 -> x1, Pallas kernels: none -> 69.7 us  [local(): pl.pallas_call(functools.partial(context_kernel, n, kv_heads, per_group,...]
    dot_general x8 -> x0, matrix products: 31.4 us -> none  [the longest x4 18 us: attend(): lax.dot_general(weights, value_block, (((2,), (0,)), ((0,), (1,))), prefe...]
    all_to_all x1 -> x0, waiting for transfers between devices: 25.7 us -> none  [local(): lax.all_to_all(outgoing, 'ctx', split_axis=1, concat_axis=1, tiled=True)]
    reduce_sum x8 -> x0, other arithmetic: 11.1 us -> none  [the longest x4 10.1 us: attend(): new_sum = acc_sum * correct + jnp.sum(exp_scores, axis=2)]
    while x36 -> x0, local copies, waits for them, and re-layouts: 9.48 us -> none
    all_to_all x1 -> x0, starting transfers between devices: 6.32 us -> none  [local(): lax.all_to_all(outgoing, 'ctx', split_axis=1, concat_axis=1, tiled=True)]
    slice x4 -> x0, local copies, waits for them, and re-layouts: 5.31 us -> none  [attend(): key_block = kv_piece[0].reshape(row_count, kv_heads, head_dim)]
  transfers between devices with their start and end apart: 2 -> 0, of which waited for: 2 -> 0; matrix products, arithmetic and copies ran while one was open for 1% -> 0% of each run, Pallas kernels for 0% -> 0%
where the time goes in v1:
time: 74.6 us; the launch traced here: 74.3 us
  Pallas kernels  69.7 us (93%)
  local copies, waits for them, and re-layouts  4.62 us (6%)
    pallas_call x1, Pallas kernels, local(): pl.pallas_call(functools.partial(context_kernel, n, kv_heads, per_group,...  69.7 us
    unnamed x9, local copies, waits for them, and re-layouts  4.62 us

profile of v1, /device:TPU:0, one launch (start us, length us, event | category | flops | bytes accessed | tf_op | source)
XLA Modules:
  0.0 74.3 jit_solution(9622565233395366252)
XLA Ops:
  0.0 0.0 copy-start
  0.0 1.2 %copy-done = bf16[2,8,128,256]{3,2,1,0:T(8,128)(2,1)S(1)} copy-done((bf16[2,8,128,256]{3,2,1,0:T(8,128)(2,1)S(1)}, bf16[2,8,128,256]{3,2,1,0:T(8,128)(2,1)}, u32[]{:S(2)}) %copy-start) | copy-done | bytes 1048600
  1.2 0.0 copy-start.1
  1.2 1.0 %copy-done.1 = bf16[128,2048]{1,0:T(8,128)(2,1)S(1)} copy-done((bf16[128,2048]{1,0:T(8,128)(2,1)S(1)}, bf16[128,2048]{1,0:T(8,128)(2,1)}, u32[]{:S(2)}) %copy-start.1) | copy-done | bytes 524312
  2.3 0.0 copy-start.2
  2.3 0.9 %copy-done.2 = bf16[2,128,256]{2,1,0:T(8,128)(2,1)S(1)} copy-done((bf16[2,128,256]{2,1,0:T(8,128)(2,1)S(1)}, bf16[2,128,256]{2,1,0:T(8,128)(2,1)}, u32[]{:S(2)}) %copy-start.2) | copy-done | bytes 131096
  3.2 0.0 copy-start.3
  3.2 0.7 copy-done.3
  3.8 69.7 %context_attention.1 = bf16[128,2048]{1,0:T(8,128)(2,1)S(1)} custom-call(s32[4]{0:T(128)S(1)} %copy-done.3, bf16[128,2048]{1,0:T(8,128)(2,1)S(1)} %copy-done.1, bf16[2,128,256]{2,1,0:T(8,128)(2,1)S(1)} %copy-done.2, bf16[2,8,128,256]{3,2,1,0:T(8,128)(2,1)S(1)} %copy-done), custom_call_target="tpu_custom_call" | custom-call | flops 4831838208 | bytes 1048576 | tf_op jit(solution)/shard_map/context_attention/pallas_call | solution.py:464
  73.5 0.8 %copy.6 = bf16[128,2048]{1,0:T(8,128)(2,1)} copy(bf16[128,2048]{1,0:T(8,128)(2,1)S(1)} %context_attention.1) | data formatting | bytes 1048576
Async XLA Ops:
  0.0 1.2 %copy-start = (bf16[2,8,128,256]{3,2,1,0:T(8,128)(2,1)S(1)}, bf16[2,8,128,256]{3,2,1,0:T(8,128)(2,1)}, u32[]{:S(2)}) copy-start(bf16[2,8,128,256]{3,2,1,0:T(8,128)(2,1)} %pool_ref.1) | copy-start | bytes 3145732
  1.2 1.0 %copy-start.1 = (bf16[128,2048]{1,0:T(8,128)(2,1)S(1)}, bf16[128,2048]{1,0:T(8,128)(2,1)}, u32[]{:S(2)}) copy-start(bf16[128,2048]{1,0:T(8,128)(2,1)} %queries_ref.1) | copy-start | bytes 1572868
  2.3 0.9 %copy-start.2 = (bf16[2,128,256]{2,1,0:T(8,128)(2,1)S(1)}, bf16[2,128,256]{2,1,0:T(8,128)(2,1)}, u32[]{:S(2)}) copy-start(bf16[2,128,256]{2,1,0:T(8,128)(2,1)} %new_ref.1) | copy-start | bytes 393220
  3.2 0.7 copy-start.3

commit v2 on v1

--- a/solution.py
+++ b/solution.py
@@ -271,8 +271,9 @@
     for head in range(per_group if offload else 0, kv_heads * per_group):
         query_loads[head].wait()
 
-    acc[...] = jnp.zeros(acc.shape, jnp.float32)
-    row_max[...] = jnp.full(row_max.shape, masked_score, jnp.float32)
+    if offload:
+        acc[kv_heads] = jnp.zeros(acc.shape[1:], jnp.float32)
+        row_max[kv_heads] = jnp.full(row_max.shape[1:], masked_score, jnp.float32)
 
     query_row = lax.broadcasted_iota(jnp.int32, (tile_heads, rows, block_len), 1).reshape(
         tile_rows, block_len
@@ -280,13 +281,16 @@
     key_column = lax.broadcasted_iota(jnp.int32, (tile_rows, block_len), 1)
     offset = key_column - query_row
 
-    def attend_tiles(group, source, piece, asker):
-        key_rows = kv[source, piece, 0].reshape(keys, HD)
-        value_rows = kv[source, piece, 1].reshape(keys, HD)
+    def attend_tiles(group, source, piece, count, asker, fresh=False):
+        taken = pl.ds(piece, count)
+        width = count * keys
+        key_rows = kv[source, taken, 0].reshape(width, HD)
+        value_rows = kv[source, taken, 1].reshape(width, HD)
         value_ones = jnp.concatenate([value_rows, jnp.ones_like(value_rows)], axis=1)
-        has_new = lax.rem(piece, splits) == splits - 1
         limit = (span_ref[asker] - span_ref[source]) * rows
-        limit = jnp.where(has_new, limit, rows + block_len)
+        if count < splits:
+            has_new = lax.rem(piece, splits) == splits - 1
+            limit = jnp.where(has_new, limit, rows + block_len)
         allowed = offset <= limit
         for tile in range(tiles):
             heads = pl.ds(tile * tile_heads, tile_heads)
@@ -294,25 +298,29 @@
             scores = lax.dot_general(
                 query_tile, key_rows, (((1,), (1,)), ((), ())), preferred_element_type=jnp.float32
             )
-            last = jnp.where(allowed, scores[:, keys - block_len :], masked_score)
-            scores = jnp.concatenate([scores[:, : keys - block_len], last], axis=1)
+            last = jnp.where(allowed, scores[:, width - block_len :], masked_score)
+            scores = jnp.concatenate([scores[:, : width - block_len], last], axis=1)
             span = pl.ds(tile * tile_rows, tile_rows)
-            old_max = row_max[group, span]
-            new_max = jnp.maximum(old_max, jnp.max(scores, axis=1, keepdims=True))
+            new_max = jnp.max(scores, axis=1, keepdims=True)
+            if fresh:
+                new_max = jnp.broadcast_to(new_max, (tile_rows, HD))
+            else:
+                old_max = row_max[group, span]
+                new_max = jnp.maximum(old_max, new_max)
             row_max[group, span] = new_max
-            correct = jnp.exp2((old_max - new_max) * unit)
-            wide = jnp.concatenate([new_max] * group_blocks, axis=1)
+            wide = jnp.concatenate([new_max] * (width // HD), axis=1)
             weights = jnp.exp2((scores - wide) * unit).astype(jnp.bfloat16)
             update = jnp.dot(weights, value_ones, preferred_element_type=jnp.float32)
-            acc[group, span] = (
-                acc[group, span] * jnp.concatenate([correct, correct], axis=1) + update
-            )
-
-    def own_piece(piece, carry):
-        attend_tiles(piece // splits, me, piece, me)
+            if not fresh:
+                correct = jnp.exp2((old_max - new_max) * unit)
+                update += acc[group, span] * jnp.concatenate([correct, correct], axis=1)
+            acc[group, span] = update
+
+    def own_head(head, carry):
+        attend_tiles(head, me, head * splits, splits, me, fresh=True)
         return carry
 
-    lax.fori_loop(0, pieces, own_piece, 0)
+    lax.fori_loop(0, kv_heads, own_head, 0)
 
     if offload:
 
@@ -340,44 +348,74 @@
         edge_copy(2, part_stat, got_stat, outer).start()
 
     def arrival(step, carry):
-        distance = 1 + step // (2 * pieces)
-        piece = (step % (2 * pieces)) // 2
-        side = step % 2
-        source = me + (1 - 2 * side) * distance
-        onward = me + 2 * side - 1
-        valid = (source >= 0) & (source < n)
-        has_next = (onward >= 0) & (onward < n)
-        if offload:
-            head_off = piece < splits
-            valid = valid & jnp.logical_not(at_edge & head_off & (distance >= 2))
-            handed = has_next & head_off & ((onward == 0) | (onward == n - 1))
-        else:
+        distance = 1 + step // kv_heads
+        head = step % kv_heads
+
+        def about(side):
+            source = me + (1 - 2 * side) * distance
+            onward = me + 2 * side - 1
+            valid = (source >= 0) & (source < n)
+            has_next = (onward >= 0) & (onward < n)
+            late = (distance >= 2) & (head == kv_heads - 1) & ((source == 0) | (source == n - 1))
             handed = False
-
-        @pl.when(valid)
-        def _():
+            if offload:
+                valid = valid & jnp.logical_not(at_edge & (head == 0) & (distance >= 2))
+                handed = has_next & (head == 0) & ((onward == 0) | (onward == n - 1))
+            return source, onward, valid, late, has_next & jnp.logical_not(handed), handed
+
+        def pass_on(piece, side, source, forward):
             copy = piece_copy(source, piece, side)
             copy.wait_recv()
 
-            @pl.when(has_next & jnp.logical_not(handed))
+            @pl.when(forward)
             def _():
                 copy.start()
 
-            if offload:
-
-                @pl.when(handed)
+        def one_split(split, carry):
+            for side in range(2):
+                source, _, valid, late, forward, _ = about(side)
+
+                @pl.when(valid & jnp.logical_not(late))
                 def _():
-                    attend_tiles(kv_heads, source, piece, onward)
-
-                    @pl.when((distance == n - 2) & (piece == splits - 1))
+                    pass_on(head * splits + split, side, source, forward)
+
+            return carry
+
+        lax.fori_loop(0, splits, one_split, 0)
+
+        def one_side(side, carry):
+            source, onward, valid, late, forward, handed = about(side)
+
+            @pl.when(valid & jnp.logical_not(late))
+            def _():
+                if offload:
+
+                    @pl.when(handed)
                     def _():
-                        return_part()
-
-            attend_tiles(piece // splits, source, piece, me)
-
+                        attend_tiles(kv_heads, source, head * splits, splits, onward)
+
+                        @pl.when(distance == n - 2)
+                        def _():
+                            return_part()
+
+                attend_tiles(head, source, head * splits, splits, me)
+
+            @pl.when(valid & late)
+            def _():
+                def one_late(split, carry):
+                    piece = head * splits + split
+                    pass_on(piece, side, source, forward)
+                    attend_tiles(head, source, piece, 1, me)
+                    return carry
+
+                lax.fori_loop(0, splits, one_late, 0)
+
+            return carry
+
+        lax.fori_loop(0, 2, one_side, 0)
         return carry
 
-    lax.fori_loop(0, 2 * pieces * (n - 1), arrival, 0)
+    lax.fori_loop(0, kv_heads * (n - 1), arrival, 0)
 
     def settle(group, head):
         columns = pl.ds((group * per_group + head) * HD, HD)
@@ -488,7 +526,7 @@
             pltpu.SemaphoreType.DMA((3,)),
         ],
         compiler_params=pltpu.CompilerParams(
-            collective_id=0, has_side_effects=True, vmem_limit_bytes=40 * 1024 * 1024
+            collective_id=0, has_side_effects=True, vmem_limit_bytes=60 * 1024 * 1024
         ),
         cost_estimate=pl.CostEstimate(
             flops=4 * work, bytes_accessed=4 * queries.size, transcendentals=work // HD

time: 74.6 us -> 72.3 us (0.969)
  local copies, waits for them, and re-layouts: 4.62 us -> 1.88 us
    unnamed x9 -> x1, local copies, waits for them, and re-layouts: 4.62 us -> 1.88 us
where the time goes in v2:
time: 72.3 us; the launch traced here: 72.2 us
  Pallas kernels  70.3 us (97%)
  local copies, waits for them, and re-layouts  1.88 us (3%)
    pallas_call x1, Pallas kernels, local(): pl.pallas_call(functools.partial(context_kernel, n, kv_heads, per_group,...  70.3 us
    unnamed x1, local copies, waits for them, and re-layouts  1.88 us

profile of v2, /device:TPU:0, one launch (start us, length us, event | category | flops | bytes accessed | tf_op | source)
XLA Modules:
  0.0 72.2 jit_solution(9475663840269927429)
XLA Ops:
  0.0 70.3 %context_attention.1 = bf16[128,2048]{1,0:T(8,128)(2,1)} custom-call(s32[4]{0:T(128)} %span_ref.1, bf16[128,2048]{1,0:T(8,128)(2,1)} %queries_ref.1, bf16[2,128,256]{2,1,0:T(8,128)(2,1)} %new_ref.1, bf16[2,8,128,256]{3,2,1,0:T(8,128)(2,1)} %pool_ref.1), custom_call_target="tpu_custom_call" | custom-call | flops 4831838208 | bytes 1048576 | tf_op jit(solution)/shard_map/context_attention/pallas_call | solution.py:502
  70.3 1.9 %copy.6 = bf16[128,2048]{1,0:T(8,128)(2,1)} copy(bf16[128,2048]{1,0:T(8,128)(2,1)} %context_attention.1) | data formatting | bytes 1048576

commit v3 on v0

--- a/solution.py
+++ b/solution.py
@@ -1,8 +1,11 @@
+import functools
 import math
 
 import jax
 import jax.numpy as jnp
 from jax import lax
+from jax.experimental import pallas as pl
+from jax.experimental.pallas import tpu as pltpu
 from jax.sharding import PartitionSpec as P
 
 HD = 128
@@ -73,7 +76,7 @@
     return final_state
 
 
-def local(queries, new_kv, pool, block_table, span_order):
+def routed(queries, new_kv, pool, block_table, span_order):
     cycle_size = lax.axis_size("ctx")
     my_index = lax.axis_index("ctx")
     per_group = QH // KVH
@@ -141,6 +144,378 @@
     return result.astype(jnp.bfloat16)
 
 
+def context_kernel(
+    n, kv_heads, per_group, splits,
+    span_ref, queries_ref, new_ref, pool_ref, out_ref,
+    kv, qs, acc, row_max, part_out, part_stat, got_out, got_stat,
+    load_sem, query_sem, kv_send, kv_recv, ask_send, ask_recv,
+    part_send, part_recv, stat_send, stat_recv,
+):
+    me = lax.axis_index("ctx")
+    at_edge = (me == 0) | (me == n - 1)
+    inner = jnp.logical_not(at_edge)
+    mate = jnp.where(me % 2 == 0, me + 1, me - 1)
+    across = n - 1 - me
+    far = n - 1 - mate
+    helper = jnp.where(at_edge, far, across)
+    my_role = jnp.where(at_edge, 2, 1)
+    pool_dev, block_len = pool_ref.shape[1], pool_ref.shape[2]
+    pieces, group_blocks = kv.shape[1], kv.shape[3]
+    keys = group_blocks * block_len
+    rows = queries_ref.shape[0]
+    tile_heads = 2 if per_group % 2 == 0 else 1
+    tile_rows = tile_heads * rows
+    tiles = per_group // tile_heads
+    unit = math.log2(math.e) / math.sqrt(HD)
+    MESH = pl.DeviceIdType.MESH
+
+    def asker_of(role):
+        return jnp.where(role == 0, me, jnp.where(role == 1, across, far))
+
+    loads = [[] for _ in range(pieces)]
+    count = 0
+    for piece in range(pieces):
+        kv_head, split = divmod(piece, splits)
+        columns = pl.ds(kv_head * HD, HD)
+        first = split * group_blocks
+        pool_blocks = min(group_blocks, pool_dev - first)
+        for t in range(2):
+            if pool_blocks > 0:
+                loads[piece].append(
+                    pltpu.make_async_copy(
+                        pool_ref.at[t, pl.ds(first, pool_blocks), :, columns],
+                        kv.at[0, piece, t, pl.ds(0, pool_blocks)],
+                        load_sem.at[count],
+                    )
+                )
+                count += 1
+            if pool_blocks < group_blocks:
+                loads[piece].append(
+                    pltpu.make_async_copy(
+                        new_ref.at[t, :, columns],
+                        kv.at[0, piece, t, group_blocks - 1],
+                        load_sem.at[count],
+                    )
+                )
+                count += 1
+    for piece in range(pieces):
+        for load in loads[piece]:
+            load.start()
+    query_loads = []
+    for head in range(kv_heads):
+        for member in range(per_group):
+            query_loads.append(
+                pltpu.make_async_copy(
+                    queries_ref.at[:, pl.ds((head * per_group + member) * HD, HD)],
+                    qs.at[0, head, member],
+                    query_sem.at[head * per_group + member],
+                )
+            )
+            query_loads[-1].start()
+
+    barrier = pltpu.get_barrier_semaphore()
+    pl.semaphore_signal(barrier, inc=1, device_id={"ctx": mate}, device_id_type=MESH)
+    pl.semaphore_signal(barrier, inc=1, device_id={"ctx": helper}, device_id_type=MESH)
+
+    @pl.when(inner)
+    def _():
+        pl.semaphore_signal(barrier, inc=1, device_id={"ctx": far}, device_id_type=MESH)
+        pl.semaphore_wait(barrier, 3)
+
+    @pl.when(at_edge)
+    def _():
+        pl.semaphore_wait(barrier, 2)
+
+    def kv_copy(piece):
+        return pltpu.make_async_remote_copy(
+            src_ref=kv.at[0, piece],
+            dst_ref=kv.at[1, piece],
+            send_sem=kv_send.at[piece],
+            recv_sem=kv_recv.at[piece],
+            device_id={"ctx": mate},
+            device_id_type=MESH,
+        )
+
+    def ask_copy(head, role):
+        return pltpu.make_async_remote_copy(
+            src_ref=qs.at[0, head],
+            dst_ref=qs.at[role, head],
+            send_sem=ask_send.at[head],
+            recv_sem=ask_recv.at[role - 1, head],
+            device_id={"ctx": helper},
+            device_id_type=MESH,
+        )
+
+    def part_copies(role, head):
+        target = jnp.where(role == 1, across, far)
+        return (
+            pltpu.make_async_remote_copy(
+                src_ref=part_out.at[role - 1, head],
+                dst_ref=got_out.at[head],
+                send_sem=part_send.at[role - 1, head],
+                recv_sem=part_recv.at[head],
+                device_id={"ctx": target},
+                device_id_type=MESH,
+            ),
+            pltpu.make_async_remote_copy(
+                src_ref=part_stat.at[role - 1, head],
+                dst_ref=got_stat.at[head],
+                send_sem=stat_send.at[role - 1, head],
+                recv_sem=stat_recv.at[head],
+                device_id={"ctx": target},
+                device_id_type=MESH,
+            ),
+        )
+
+    last_head = kv_heads - 1
+    held_back = last_head * splits
+
+    def ask_all():
+        for head in range(kv_heads):
+            for load in query_loads[head * per_group : (head + 1) * per_group]:
+                load.wait()
+            ask_copy(head, my_role).start()
+
+    @pl.when(inner)
+    def _():
+        ask_all()
+
+    for piece in range(pieces):
+        for load in loads[piece]:
+            load.wait()
+        if piece < held_back:
+            kv_copy(piece).start()
+
+    @pl.when(at_edge)
+    def _():
+        ask_all()
+
+    @pl.when(inner)
+    def _():
+        for piece in range(held_back, pieces):
+            kv_copy(piece).start()
+
+    query_row = lax.broadcasted_iota(jnp.int32, (tile_heads, rows, block_len), 1).reshape(
+        tile_rows, block_len
+    )
+    key_column = lax.broadcasted_iota(jnp.int32, (tile_rows, block_len), 1)
+    offset = key_column - query_row
+
+    def attend_tiles(role, head, slot, split, count, fresh=False):
+        taken = pl.ds(head * splits + split, count)
+        width = count * keys
+        key_rows = kv[slot, taken, 0].reshape(width, HD)
+        value_rows = kv[slot, taken, 1].reshape(width, HD)
+        value_ones = jnp.concatenate([value_rows, jnp.ones_like(value_rows)], axis=1)
+        limit = (span_ref[asker_of(role)] - span_ref[jnp.where(slot == 0, me, mate)]) * rows
+        if count < splits:
+            has_new = split == splits - 1
+            limit = jnp.where(has_new, limit, rows + block_len)
+        allowed = offset <= limit
+        for tile in range(tiles):
+            heads = pl.ds(tile * tile_heads, tile_heads)
+            query_tile = qs[role, head, heads].reshape(tile_rows, HD)
+            scores = lax.dot_general(
+                query_tile, key_rows, (((1,), (1,)), ((), ())), preferred_element_type=jnp.float32
+            )
+            last = jnp.where(allowed, scores[:, width - block_len :], masked_score)
+            scores = jnp.concatenate([scores[:, : width - block_len], last], axis=1)
+            span = pl.ds(tile * tile_rows, tile_rows)
+            new_max = jnp.max(scores, axis=1, keepdims=True)
+            if fresh:
+                new_max = jnp.broadcast_to(new_max, (tile_rows, HD))
+            else:
+                old_max = row_max[role, head, span]
+                new_max = jnp.maximum(old_max, new_max)
+            row_max[role, head, span] = new_max
+            wide = jnp.concatenate([new_max] * (width // HD), axis=1)
+            weights = jnp.exp2((scores - wide) * unit).astype(jnp.bfloat16)
+            update = jnp.dot(weights, value_ones, preferred_element_type=jnp.float32)
+            if not fresh:
+                correct = jnp.exp2((old_max - new_max) * unit)
+                update += acc[role, head, span] * jnp.concatenate([correct, correct], axis=1)
+            acc[role, head, span] = update
+
+    diagonal = lax.broadcasted_iota(jnp.int32, (rows, HD), 0) == lax.broadcasted_iota(
+        jnp.int32, (rows, HD), 1
+    )
+
+    def return_part(role, head):
+        for member in range(per_group):
+            span = pl.ds(member * rows, rows)
+            total = acc[role, head, span, HD:]
+            part_out[role - 1, head, member] = (acc[role, head, span, :HD] / total).astype(
+                jnp.bfloat16
+            )
+            peak = row_max[role, head, span]
+            part_stat[role - 1, head, 0, pl.ds(member, 1)] = jnp.sum(
+                jnp.where(diagonal, peak, 0.0), axis=0, keepdims=True
+            )
+            part_stat[role - 1, head, 1, pl.ds(member, 1)] = jnp.sum(
+                jnp.where(diagonal, total, 0.0), axis=0, keepdims=True
+            )
+        for copy in part_copies(role, head):
+            copy.start()
+
+    def near_keys(step, carry):
+        role, head = step // kv_heads, step % kv_heads
+
+        @pl.when((role == 0) | inner)
+        def _():
+            @pl.when(role == 1)
+            def _():
+                ask_copy(head, 1).wait_recv()
+
+            attend_tiles(role, head, 0, 0, splits, fresh=True)
+
+        return carry
+
+    lax.fori_loop(0, 2 * kv_heads, near_keys, 0)
+
+    @pl.when(at_edge)
+    def _():
+        for piece in range(held_back):
+            kv_copy(piece).wait_send()
+        for piece in range(held_back, pieces):
+            kv_copy(piece).start()
+
+    for head in range(last_head):
+        for split in range(splits):
+            kv_copy(head * splits + split).wait_recv()
+
+        def one_role(step, carry, head=head):
+            role = (step + 1) % 3
+
+            @pl.when((role == 0) | inner)
+            def _():
+                @pl.when(role == 2)
+                def _():
+                    ask_copy(head, 2).wait_recv()
+                    attend_tiles(role, head, 0, 0, splits, fresh=True)
+
+                attend_tiles(role, head, 1, 0, splits)
+
+                @pl.when(role > 0)
+                def _():
+                    return_part(role, head)
+
+            return carry
+
+        lax.fori_loop(0, 3, one_role, 0)
+
+    @pl.when(inner)
+    def _():
+        ask_copy(last_head, 2).wait_recv()
+        attend_tiles(2, last_head, 0, 0, splits, fresh=True)
+
+    def last_pieces(step, carry):
+        split, role = step // 3, (step + 1) % 3
+
+        @pl.when(role == 1)
+        def _():
+            kv_copy(held_back + split).wait_recv()
+
+        @pl.when((role == 0) | inner)
+        def _():
+            attend_tiles(role, last_head, 1, split, 1)
+
+            @pl.when((role > 0) & (split == splits - 1))
+            def _():
+                return_part(role, last_head)
+
+        return carry
+
+    lax.fori_loop(0, 3 * splits, last_pieces, 0)
+
+    def settle(head, member):
+        span = pl.ds(member * rows, rows)
+        their_max = jnp.broadcast_to(got_stat[head, 0, pl.ds(member, 1)], (HD, rows)).T
+        their_total = jnp.broadcast_to(got_stat[head, 1, pl.ds(member, 1)], (HD, rows)).T
+        my_max = row_max[0, head, span]
+        top = jnp.maximum(my_max, their_max)
+        mine = jnp.exp2((my_max - top) * unit)
+        theirs = jnp.exp2((their_max - top) * unit) * their_total
+        total = acc[0, head, span, HD:] * mine + theirs
+        summed = acc[0, head, span, :HD] * mine + got_out[head, member].astype(jnp.float32) * theirs
+        columns = pl.ds((head * per_group + member) * HD, HD)
+        out_ref[:, columns] = (summed / total).astype(out_ref.dtype)
+
+    for head in range(kv_heads):
+        for copy in part_copies(my_role, head):
+            copy.wait_recv()
+        for member in range(per_group):
+            settle(head, member)
+
+    @pl.when(inner)
+    def _():
+        for piece in range(held_back):
+            kv_copy(piece).wait_send()
+        for role in (1, 2):
+            for head in range(kv_heads):
+                for copy in part_copies(role, head):
+                    copy.wait_send()
+
+    for piece in range(held_back, pieces):
+        kv_copy(piece).wait_send()
+    for head in range(kv_heads):
+        ask_copy(head, my_role).wait_send()
+
+
+def local(queries, new_kv, pool, block_table, span_order):
+    n = lax.axis_size("ctx")
+    pool_dev, block_len = pool.shape[1], pool.shape[2]
+    rows = queries.shape[0]
+    kv_heads = new_kv.shape[2] // HD
+    per_group = QH // KVH
+    whole_pool = block_table.shape[0] == n * pool_dev
+    if not whole_pool or n != 4 or rows != block_len or rows != HD:
+        return routed(queries, new_kv, pool, block_table, span_order)
+    blocks = pool_dev + 1
+    splits = 3 if blocks % 3 == 0 and blocks > 3 else 1
+    pieces = kv_heads * splits
+    group_blocks = blocks // splits
+    group_rows = per_group * rows
+    work = queries.shape[1] * rows * block_len * blocks * n
+    return pl.pallas_call(
+        functools.partial(context_kernel, n, kv_heads, per_group, splits),
+        out_shape=jax.ShapeDtypeStruct(queries.shape, jnp.bfloat16),
+        in_specs=[
+            pl.BlockSpec(memory_space=pltpu.SMEM),
+            pl.BlockSpec(memory_space=pl.ANY),
+            pl.BlockSpec(memory_space=pl.ANY),
+            pl.BlockSpec(memory_space=pl.ANY),
+        ],
+        out_specs=pl.BlockSpec(memory_space=pltpu.VMEM),
+        scratch_shapes=[
+            pltpu.VMEM((2, pieces, 2, group_blocks, block_len, HD), jnp.bfloat16),
+            pltpu.VMEM((3, kv_heads, per_group, rows, HD), jnp.bfloat16),
+            pltpu.VMEM((3, kv_heads, group_rows, 2 * HD), jnp.float32),
+            pltpu.VMEM((3, kv_heads, group_rows, HD), jnp.float32),
+            pltpu.VMEM((2, kv_heads, per_group, rows, HD), jnp.bfloat16),
+            pltpu.VMEM((2, kv_heads, 2, per_group, HD), jnp.float32),
+            pltpu.VMEM((kv_heads, per_group, rows, HD), jnp.bfloat16),
+            pltpu.VMEM((kv_heads, 2, per_group, HD), jnp.float32),
+            pltpu.SemaphoreType.DMA((4 * pieces,)),
+            pltpu.SemaphoreType.DMA((kv_heads * per_group,)),
+            pltpu.SemaphoreType.DMA((pieces,)),
+            pltpu.SemaphoreType.DMA((pieces,)),
+            pltpu.SemaphoreType.DMA((kv_heads,)),
+            pltpu.SemaphoreType.DMA((2, kv_heads)),
+            pltpu.SemaphoreType.DMA((2, kv_heads)),
+            pltpu.SemaphoreType.DMA((kv_heads,)),
+            pltpu.SemaphoreType.DMA((2, kv_heads)),
+            pltpu.SemaphoreType.DMA((kv_heads,)),
+        ],
+        compiler_params=pltpu.CompilerParams(
+            collective_id=0, has_side_effects=True, vmem_limit_bytes=60 * 1024 * 1024
+        ),
+        cost_estimate=pl.CostEstimate(
+            flops=4 * work, bytes_accessed=4 * queries.size, transcendentals=work // HD
+        ),
+        name="context_attention",
+    )(span_order, queries, new_kv, pool)
+
+
 def solution(mesh):
     return jax.shard_map(
         local,

time: 203 us -> 61.3 us (0.30)
  waiting for transfers between devices: 111 us -> 0 us
  Pallas kernels: 0 us -> 59.2 us
  matrix products: 31.4 us -> 0 us
  local copies, waits for them, and re-layouts: 22.3 us -> 1.88 us
  other arithmetic: 17.5 us -> 0 us
  between operations: 14.2 us -> 0.01 us
  starting transfers between devices: 6.32 us -> 0 us
    all_gather x1 -> x0, waiting for transfers between devices: 85.1 us -> none  [local(): kv_piece = lax.all_gather(resident, 'ctx', axis=1, tiled=True)]
    pallas_call x0 -> x1, Pallas kernels: none -> 59.2 us  [local(): pl.pallas_call(functools.partial(context_kernel, n, kv_heads, per_group,...]
    dot_general x8 -> x0, matrix products: 31.4 us -> none  [the longest x4 18 us: attend(): lax.dot_general(weights, value_block, (((2,), (0,)), ((0,), (1,))), prefe...]
    all_to_all x1 -> x0, waiting for transfers between devices: 25.7 us -> none  [local(): lax.all_to_all(outgoing, 'ctx', split_axis=1, concat_axis=1, tiled=True)]
    reduce_sum x8 -> x0, other arithmetic: 11.1 us -> none  [the longest x4 10.1 us: attend(): new_sum = acc_sum * correct + jnp.sum(exp_scores, axis=2)]
    while x36 -> x0, local copies, waits for them, and re-layouts: 9.48 us -> none
    all_to_all x1 -> x0, starting transfers between devices: 6.32 us -> none  [local(): lax.all_to_all(outgoing, 'ctx', split_axis=1, concat_axis=1, tiled=True)]
    slice x4 -> x0, local copies, waits for them, and re-layouts: 5.31 us -> none  [attend(): key_block = kv_piece[0].reshape(row_count, kv_heads, head_dim)]
  transfers between devices with their start and end apart: 2 -> 0, of which waited for: 2 -> 0; matrix products, arithmetic and copies ran while one was open for 1% -> 0% of each run, Pallas kernels for 0% -> 0%
where the time goes in v3:
time: 61.3 us; the launch traced here: 61.1 us
  Pallas kernels  59.2 us (97%)
  local copies, waits for them, and re-layouts  1.88 us (3%)
    pallas_call x1, Pallas kernels, local(): pl.pallas_call(functools.partial(context_kernel, n, kv_heads, per_group,...  59.2 us
    unnamed x1, local copies, waits for them, and re-layouts  1.88 us

profile of v3, /device:TPU:0, one launch (start us, length us, event | category | flops | bytes accessed | tf_op | source)
XLA Modules:
  0.0 61.1 jit_solution(8477151340605591524)
XLA Ops:
  0.0 59.2 %context_attention.1 = bf16[128,2048]{1,0:T(8,128)(2,1)} custom-call(s32[4]{0:T(128)} %span_ref.1, bf16[128,2048]{1,0:T(8,128)(2,1)} %queries_ref.1, bf16[2,128,256]{2,1,0:T(8,128)(2,1)} %new_ref.1, bf16[2,8,128,256]{3,2,1,0:T(8,128)(2,1)} %pool_ref.1), custom_call_target="tpu_custom_call" | custom-call | flops 4831838208 | bytes 1048576 | tf_op jit(solution)/shard_map/context_attention/pallas_call | solution.py:479
  59.2 1.9 %copy.6 = bf16[128,2048]{1,0:T(8,128)(2,1)} copy(bf16[128,2048]{1,0:T(8,128)(2,1)} %context_attention.1) | data formatting | bytes 1048576

commit v4 on v3

--- a/solution.py
+++ b/solution.py
@@ -146,9 +146,10 @@
 
 def context_kernel(
     n, kv_heads, per_group, splits,
-    span_ref, queries_ref, new_ref, pool_ref, out_ref,
+    order_ref, queries_ref, new_ref, pool_ref, out_ref,
+    span_ref,
     kv, qs, acc, row_max, part_out, part_stat, got_out, got_stat,
-    load_sem, query_sem, kv_send, kv_recv, ask_send, ask_recv,
+    order_sem, load_sem, query_sem, kv_send, kv_recv, ask_send, ask_recv,
     part_send, part_recv, stat_send, stat_recv,
 ):
     me = lax.axis_index("ctx")
@@ -166,6 +167,8 @@
     tile_heads = 2 if per_group % 2 == 0 else 1
     tile_rows = tile_heads * rows
     tiles = per_group // tile_heads
+    halves = part_out.shape[2]
+    half_heads = per_group // halves
     unit = math.log2(math.e) / math.sqrt(HD)
     MESH = pl.DeviceIdType.MESH
 
@@ -201,6 +204,8 @@
     for piece in range(pieces):
         for load in loads[piece]:
             load.start()
+    order_load = pltpu.make_async_copy(order_ref, span_ref, order_sem)
+    order_load.start()
     query_loads = []
     for head in range(kv_heads):
         for member in range(per_group):
@@ -246,22 +251,22 @@
             device_id_type=MESH,
         )
 
-    def part_copies(role, head):
+    def part_copies(role, head, half):
         target = jnp.where(role == 1, across, far)
         return (
             pltpu.make_async_remote_copy(
-                src_ref=part_out.at[role - 1, head],
-                dst_ref=got_out.at[head],
-                send_sem=part_send.at[role - 1, head],
-                recv_sem=part_recv.at[head],
+                src_ref=part_out.at[role - 1, head, half],
+                dst_ref=got_out.at[head, half],
+                send_sem=part_send.at[role - 1, head, half],
+                recv_sem=part_recv.at[head, half],
                 device_id={"ctx": target},
                 device_id_type=MESH,
             ),
             pltpu.make_async_remote_copy(
-                src_ref=part_stat.at[role - 1, head],
-                dst_ref=got_stat.at[head],
-                send_sem=stat_send.at[role - 1, head],
-                recv_sem=stat_recv.at[head],
+                src_ref=part_stat.at[role - 1, head, half],
+                dst_ref=got_stat.at[head, half],
+                send_sem=stat_send.at[role - 1, head, half],
+                recv_sem=stat_recv.at[head, half],
                 device_id={"ctx": target},
                 device_id_type=MESH,
             ),
@@ -301,7 +306,7 @@
     key_column = lax.broadcasted_iota(jnp.int32, (tile_rows, block_len), 1)
     offset = key_column - query_row
 
-    def attend_tiles(role, head, slot, split, count, fresh=False):
+    def attend_tiles(role, head, slot, split, count, fresh=False, half=None):
         taken = pl.ds(head * splits + split, count)
         width = count * keys
         key_rows = kv[slot, taken, 0].reshape(width, HD)
@@ -312,15 +317,17 @@
             has_new = split == splits - 1
             limit = jnp.where(has_new, limit, rows + block_len)
         allowed = offset <= limit
-        for tile in range(tiles):
-            heads = pl.ds(tile * tile_heads, tile_heads)
+        first_row = 0 if half is None else pl.multiple_of(half * (half_heads * rows), tile_rows)
+        first_head = 0 if half is None else half * half_heads
+        for tile in range(tiles if half is None else tiles // halves):
+            heads = pl.ds(first_head + tile * tile_heads, tile_heads)
             query_tile = qs[role, head, heads].reshape(tile_rows, HD)
             scores = lax.dot_general(
                 query_tile, key_rows, (((1,), (1,)), ((), ())), preferred_element_type=jnp.float32
             )
             last = jnp.where(allowed, scores[:, width - block_len :], masked_score)
             scores = jnp.concatenate([scores[:, : width - block_len], last], axis=1)
-            span = pl.ds(tile * tile_rows, tile_rows)
+            span = pl.ds(first_row + tile * tile_rows, tile_rows)
             new_max = jnp.max(scores, axis=1, keepdims=True)
             if fresh:
                 new_max = jnp.broadcast_to(new_max, (tile_rows, HD))
@@ -340,22 +347,25 @@
         jnp.int32, (rows, HD), 1
     )
 
-    def return_part(role, head):
-        for member in range(per_group):
-            span = pl.ds(member * rows, rows)
+    def return_part(role, head, half):
+        for member in range(half_heads):
+            first = (half * half_heads + member) * rows
+            span = pl.ds(pl.multiple_of(first, rows), rows)
             total = acc[role, head, span, HD:]
-            part_out[role - 1, head, member] = (acc[role, head, span, :HD] / total).astype(
+            part_out[role - 1, head, half, member] = (acc[role, head, span, :HD] / total).astype(
                 jnp.bfloat16
             )
             peak = row_max[role, head, span]
-            part_stat[role - 1, head, 0, pl.ds(member, 1)] = jnp.sum(
+            part_stat[role - 1, head, half, pl.ds(member, 1)] = jnp.sum(
                 jnp.where(diagonal, peak, 0.0), axis=0, keepdims=True
             )
-            part_stat[role - 1, head, 1, pl.ds(member, 1)] = jnp.sum(
+            part_stat[role - 1, head, half, pl.ds(half_heads + member, 1)] = jnp.sum(
                 jnp.where(diagonal, total, 0.0), axis=0, keepdims=True
             )
-        for copy in part_copies(role, head):
+        for copy in part_copies(role, head, half):
             copy.start()
+
+    order_load.wait()
 
     def near_keys(step, carry):
         role, head = step // kv_heads, step % kv_heads
@@ -397,7 +407,11 @@
 
                 @pl.when(role > 0)
                 def _():
-                    return_part(role, head)
+                    def one_half(half, carry):
+                        return_part(role, head, half)
+                        return carry
+
+                    lax.fori_loop(0, halves, one_half, 0)
 
             return carry
 
@@ -417,34 +431,43 @@
 
         @pl.when((role == 0) | inner)
         def _():
-            attend_tiles(role, last_head, 1, split, 1)
-
-            @pl.when((role > 0) & (split == splits - 1))
-            def _():
-                return_part(role, last_head)
+            def one_half(half, carry):
+                attend_tiles(role, last_head, 1, split, 1, half=half)
+
+                @pl.when((role > 0) & (split == splits - 1))
+                def _():
+                    return_part(role, last_head, half)
+
+                return carry
+
+            lax.fori_loop(0, halves, one_half, 0)
 
         return carry
 
     lax.fori_loop(0, 3 * splits, last_pieces, 0)
 
-    def settle(head, member):
-        span = pl.ds(member * rows, rows)
-        their_max = jnp.broadcast_to(got_stat[head, 0, pl.ds(member, 1)], (HD, rows)).T
-        their_total = jnp.broadcast_to(got_stat[head, 1, pl.ds(member, 1)], (HD, rows)).T
+    def settle(head, half, member):
+        index = half * half_heads + member
+        span = pl.ds(index * rows, rows)
+        their_max = jnp.broadcast_to(got_stat[head, half, pl.ds(member, 1)], (HD, rows)).T
+        their_total = jnp.broadcast_to(
+            got_stat[head, half, pl.ds(half_heads + member, 1)], (HD, rows)
+        ).T
         my_max = row_max[0, head, span]
         top = jnp.maximum(my_max, their_max)
         mine = jnp.exp2((my_max - top) * unit)
         theirs = jnp.exp2((their_max - top) * unit) * their_total
         total = acc[0, head, span, HD:] * mine + theirs
-        summed = acc[0, head, span, :HD] * mine + got_out[head, member].astype(jnp.float32) * theirs
-        columns = pl.ds((head * per_group + member) * HD, HD)
+        summed = acc[0, head, span, :HD] * mine + got_out[head, half, member].astype(jnp.float32) * theirs
+        columns = pl.ds((head * per_group + index) * HD, HD)
         out_ref[:, columns] = (summed / total).astype(out_ref.dtype)
 
     for head in range(kv_heads):
-        for copy in part_copies(my_role, head):
-            copy.wait_recv()
-        for member in range(per_group):
-            settle(head, member)
+        for half in range(halves):
+            for copy in part_copies(my_role, head, half):
+                copy.wait_recv()
+            for member in range(half_heads):
+                settle(head, half, member)
 
     @pl.when(inner)
     def _():
@@ -452,8 +475,9 @@
             kv_copy(piece).wait_send()
         for role in (1, 2):
             for head in range(kv_heads):
-                for copy in part_copies(role, head):
-                    copy.wait_send()
+                for half in range(halves):
+                    for copy in part_copies(role, head, half):
+                        copy.wait_send()
 
     for piece in range(held_back, pieces):
         kv_copy(piece).wait_send()
@@ -475,45 +499,53 @@
     pieces = kv_heads * splits
     group_blocks = blocks // splits
     group_rows = per_group * rows
+    halves = 2 if per_group % 4 == 0 else 1
     work = queries.shape[1] * rows * block_len * blocks * n
     return pl.pallas_call(
         functools.partial(context_kernel, n, kv_heads, per_group, splits),
         out_shape=jax.ShapeDtypeStruct(queries.shape, jnp.bfloat16),
         in_specs=[
-            pl.BlockSpec(memory_space=pltpu.SMEM),
-            pl.BlockSpec(memory_space=pl.ANY),
-            pl.BlockSpec(memory_space=pl.ANY),
-            pl.BlockSpec(memory_space=pl.ANY),
+            pl.BlockSpec(memory_space=pltpu.HBM),
+            pl.BlockSpec(memory_space=pltpu.HBM),
+            pl.BlockSpec(memory_space=pltpu.HBM),
+            pl.BlockSpec(memory_space=pltpu.HBM),
         ],
         out_specs=pl.BlockSpec(memory_space=pltpu.VMEM),
         scratch_shapes=[
+            pltpu.SMEM(span_order.shape, jnp.int32),
             pltpu.VMEM((2, pieces, 2, group_blocks, block_len, HD), jnp.bfloat16),
             pltpu.VMEM((3, kv_heads, per_group, rows, HD), jnp.bfloat16),
             pltpu.VMEM((3, kv_heads, group_rows, 2 * HD), jnp.float32),
             pltpu.VMEM((3, kv_heads, group_rows, HD), jnp.float32),
-            pltpu.VMEM((2, kv_heads, per_group, rows, HD), jnp.bfloat16),
-            pltpu.VMEM((2, kv_heads, 2, per_group, HD), jnp.float32),
-            pltpu.VMEM((kv_heads, per_group, rows, HD), jnp.bfloat16),
-            pltpu.VMEM((kv_heads, 2, per_group, HD), jnp.float32),
+            pltpu.VMEM((2, kv_heads, halves, per_group // halves, rows, HD), jnp.bfloat16),
+            pltpu.VMEM((2, kv_heads, halves, 2 * (per_group // halves), HD), jnp.float32),
+            pltpu.VMEM((kv_heads, halves, per_group // halves, rows, HD), jnp.bfloat16),
+            pltpu.VMEM((kv_heads, halves, 2 * (per_group // halves), HD), jnp.float32),
+            pltpu.SemaphoreType.DMA,
             pltpu.SemaphoreType.DMA((4 * pieces,)),
             pltpu.SemaphoreType.DMA((kv_heads * per_group,)),
             pltpu.SemaphoreType.DMA((pieces,)),
             pltpu.SemaphoreType.DMA((pieces,)),
             pltpu.SemaphoreType.DMA((kv_heads,)),
             pltpu.SemaphoreType.DMA((2, kv_heads)),
-            pltpu.SemaphoreType.DMA((2, kv_heads)),
-            pltpu.SemaphoreType.DMA((kv_heads,)),
-            pltpu.SemaphoreType.DMA((2, kv_heads)),
-            pltpu.SemaphoreType.DMA((kv_heads,)),
+            pltpu.SemaphoreType.DMA((2, kv_heads, halves)),
+            pltpu.SemaphoreType.DMA((kv_heads, halves)),
+            pltpu.SemaphoreType.DMA((2, kv_heads, halves)),
+            pltpu.SemaphoreType.DMA((kv_heads, halves)),
         ],
         compiler_params=pltpu.CompilerParams(
-            collective_id=0, has_side_effects=True, vmem_limit_bytes=60 * 1024 * 1024
+            collective_id=0, has_side_effects=True, vmem_limit_bytes=40 * 1024 * 1024
         ),
         cost_estimate=pl.CostEstimate(
             flops=4 * work, bytes_accessed=4 * queries.size, transcendentals=work // HD
         ),
         name="context_attention",
-    )(span_order, queries, new_kv, pool)
+    )(
+        *(
+            pltpu.with_memory_space_constraint(held, pltpu.HBM)
+            for held in (span_order, queries, new_kv, pool)
+        )
+    )
 
 
 def solution(mesh):

time: 61.3 us -> 58.2 us (0.949)
  Pallas kernels: 59.2 us -> 57.2 us
  local copies, waits for them, and re-layouts: 1.88 us -> 0.8 us
    pallas_call x1, Pallas kernels: 59.2 us -> 57.2 us  [local(): pl.pallas_call(functools.partial(context_kernel, n, kv_heads, per_group,...]
    unnamed x1, local copies, waits for them, and re-layouts: 1.88 us -> 0.8 us
where the time goes in v4:
time: 58.2 us; the launch traced here: 58 us
  Pallas kernels  57.2 us (98%)
  local copies, waits for them, and re-layouts  0.8 us (1%)
    pallas_call x1, Pallas kernels, local(): pl.pallas_call(functools.partial(context_kernel, n, kv_heads, per_group,...  57.2 us

profile of v4, /device:TPU:0, one launch (start us, length us, event | category | flops | bytes accessed | tf_op | source)
XLA Modules:
  0.0 58.0 jit_solution(15014529946368291888)
XLA Ops:
  0.0 57.2 %context_attention.1 = bf16[128,2048]{1,0:T(8,128)(2,1)S(1)} custom-call(s32[4]{0:T(128)} %order_ref.1, bf16[128,2048]{1,0:T(8,128)(2,1)} %queries_ref.1, bf16[2,128,256]{2,1,0:T(8,128)(2,1)} %new_ref.1, bf16[2,8,128,256]{3,2,1,0:T(8,128)(2,1)} %pool_ref.1), custom_call_target="tpu_custom_call" | custom-call | flops 4831838208 | bytes 1048576 | tf_op jit(solution)/shard_map/context_attention/pallas_call | solution.py:504
  57.2 0.8 %copy.6 = bf16[128,2048]{1,0:T(8,128)(2,1)} copy(bf16[128,2048]{1,0:T(8,128)(2,1)S(1)} %context_attention.1) | data formatting | bytes 1048576

commit v5 on v4

--- a/solution.py
+++ b/solution.py
@@ -499,7 +499,7 @@
     pieces = kv_heads * splits
     group_blocks = blocks // splits
     group_rows = per_group * rows
-    halves = 2 if per_group % 4 == 0 else 1
+    halves = 4 if per_group % 8 == 0 else 1
     work = queries.shape[1] * rows * block_len * blocks * n
     return pl.pallas_call(
         functools.partial(context_kernel, n, kv_heads, per_group, splits),

time: 58.2 us -> 62.2 us (1.069)
  Pallas kernels: 57.2 us -> 61.2 us
    pallas_call x1, Pallas kernels: 57.2 us -> 61.2 us  [local(): pl.pallas_call(functools.partial(context_kernel, n, kv_heads, per_group,...]
where the time goes in v5:
time: 62.2 us; the launch traced here: 62 us
  Pallas kernels  61.2 us (98%)
  local copies, waits for them, and re-layouts  0.8 us (1%)
    pallas_call x1, Pallas kernels, local(): pl.pallas_call(functools.partial(context_kernel, n, kv_heads, per_group,...  61.2 us

profile of v5, /device:TPU:0, one launch (start us, length us, event | category | flops | bytes accessed | tf_op | source)
XLA Modules:
  0.0 62.0 jit_solution(8883834610303969319)
XLA Ops:
  0.0 61.2 %context_attention.1 = bf16[128,2048]{1,0:T(8,128)(2,1)S(1)} custom-call(s32[4]{0:T(128)} %order_ref.1, bf16[128,2048]{1,0:T(8,128)(2,1)} %queries_ref.1, bf16[2,128,256]{2,1,0:T(8,128)(2,1)} %new_ref.1, bf16[2,8,128,256]{3,2,1,0:T(8,128)(2,1)} %pool_ref.1), custom_call_target="tpu_custom_call" | custom-call | flops 4831838208 | bytes 1048576 | tf_op jit(solution)/shard_map/context_attention/pallas_call | solution.py:504
  61.2 0.8 %copy.6 = bf16[128,2048]{1,0:T(8,128)(2,1)} copy(bf16[128,2048]{1,0:T(8,128)(2,1)S(1)} %context_attention.1) | data formatting | bytes 1048576
